TPU v7x, 128 devices: a whole 4x4x4 slice. The times are simulated.
128 devices in a mesh: row: 4 (over y), gz: 2 (over x_lo), vert: 16 (over z, x_hi, core).
Axes of the slice: x: 4 (x_hi: 2, x_lo: 2; x = x_hi * 2 + x_lo), y: 4, z: 4, core: 2. Of those that a mesh axis runs over, the one named last changes fastest.
Arguments:
- distribution: float32 [32, 32, 110592], P('row', 'gz', 'vert'), may hold values from 0 to 10, as said below
- z_order: int32 [48], P('vert'), may hold values from 0 to 47, as said below
- edge_codes: int32 [2, 4], P(None, 'row'), may hold values from 0 to 2, as said below
Outputs:
- new_distribution: float32 [32, 32, 110592], P('row', 'gz', 'vert')
- macroscopic: float32 [8, 32, 32], P(None, 'row', 'gz')
- boundary_flux: float32 [2, 32], P('gz', 'row')
Inputs may be any that keep to these rules, and one draw needn't show every extreme that they name: `z_order`: a permutation of 0 to 47. `edge_codes`: row 0 holds 0 (diffuse wall) or 1 (evaporating film), row 1 holds 0 (diffuse wall) or 2 (outflow); the first column's bottom is film and the last column's top is outflow. `distribution`: every entry is positive.
All inputs are finite; a program needn't handle non-finite values.
Results may differ from a plain program's by a relative error of at most 0.0003.
Values sent between devices are 32-bit elements; how exact they have to be, the bound alone decides.
A program may use at most 128 MiB of HBM per device.

v0:
```python
import math
import jax
import jax.numpy as jnp
import numpy as np
from jax import lax
from jax.sharding import PartitionSpec as P

NODES = 8
NVR = 48
NVT = 48
NVZ = 48
STEPS = 2
ELEMENT_WIDTH = 4.0
TIME_STEP = 0.001
KNUDSEN = 0.005
VISCOUS_RATIO = 2.0 / 3.0
SAT_DENSITY = 1.5
SPEED_LIMIT = 5.0
HIGHEST_PRECISION = lax.Precision.HIGHEST


def with_halo(cells, sides, width):
    for axis, dim in sides:
        count = lax.axis_size(axis)
        ends = count - 1
        head = lax.slice_in_dim(cells, 0, width, axis=dim)
        tail = lax.slice_in_dim(cells, cells.shape[dim] - width, cells.shape[dim], axis=dim)
        cells = jnp.concatenate(
            [
                lax.ppermute(tail, axis, [(i, (i + 1) % count) for i in range(ends)]),
                cells,
                lax.ppermute(head, axis, [((i + 1) % count, i) for i in range(ends)]),
            ],
            axis=dim,
        )
    return cells


def legendre_pair(position, point_count):
    previous = 1.0
    current = position
    for degree in range(2, point_count + 1):
        previous, current = (
            current,
            ((2 * degree - 1) * position * current - (degree - 1) * previous) / degree,
        )
    slope = point_count * (position * current - previous) / (position * position - 1.0)
    return (current, slope)


def dg_tables(point_count):
    point_list = []
    weight_list = []
    for number in range(point_count):
        position = math.cos(math.pi * (number + 0.75) / (point_count + 0.5))
        for sweep in range(60):
            value, slope = legendre_pair(position, point_count)
            position = position - value / slope
        value, slope = legendre_pair(position, point_count)
        point_list.append(position)
        weight_list.append(2.0 / ((1.0 - position * position) * slope * slope))
    point_list = point_list[::-1]
    weight_list = weight_list[::-1]
    products = []
    for row_number in range(point_count):
        product_value = 1.0
        for other in range(point_count):
            if other != row_number:
                product_value = product_value * (point_list[row_number] - point_list[other])
        products.append(product_value)
    derivative_rows = []
    for row_number in range(point_count):
        entries = []
        for column in range(point_count):
            if column == row_number:
                total_value = 0.0
                for other in range(point_count):
                    if other != row_number:
                        total_value = total_value + 1.0 / (
                            point_list[row_number] - point_list[other]
                        )
                entries.append(total_value)
            else:
                entries.append(
                    products[row_number]
                    / products[column]
                    / (point_list[row_number] - point_list[column])
                )
        derivative_rows.append(entries)
    right_list = []
    left_list = []
    for column in range(point_count):
        right_value = 1.0
        left_value = 1.0
        for other in range(point_count):
            if other != column:
                right_value = right_value * (1.0 - point_list[other])
                left_value = left_value * (-1.0 - point_list[other])
        right_list.append(right_value / products[column])
        left_list.append(left_value / products[column])
    points = np.array(point_list)
    quad_weights = np.array(weight_list)
    derivative = np.array(derivative_rows)
    end_right = np.array(right_list)
    end_left = np.array(left_list)
    return (
        points,
        jnp.asarray(derivative, jnp.float32),
        jnp.asarray(end_right / quad_weights, jnp.float32),
        jnp.asarray(end_left / quad_weights, jnp.float32),
        jnp.asarray(end_right, jnp.float32),
        jnp.asarray(end_left, jnp.float32),
    )


def speed_grid(point_count):
    return -SPEED_LIMIT + (np.arange(point_count) + 0.5) * (2.0 * SPEED_LIMIT / point_count)


def shift_velocity(field_entries, offset, keep_mask):
    padding = jnp.zeros(field_entries.shape[:-1] + (abs(offset),), field_entries.dtype)
    if offset > 0:
        shifted = jnp.concatenate([field_entries[..., offset:], padding], -1)
    else:
        shifted = jnp.concatenate([padding, field_entries[..., :offset]], -1)
    return jnp.where(keep_mask, shifted, 0.0)


def on_device(distribution, z_order, edge_codes):
    local_r, local_z, vdev = distribution.shape
    row_count = local_r // NODES
    col_count = local_z // NODES
    node_count = local_r * local_z
    plane_size = NVR * NVT
    slot_count = vdev // plane_size
    row_index = lax.axis_index("row")
    gz_index = lax.axis_index("gz")
    row_total = lax.axis_size("row")
    gz_total = lax.axis_size("gz")
    points, derivative, lift_right, lift_left, end_right, end_left = dg_tables(NODES)
    weight = (
        2
        * SPEED_LIMIT
        / NVR
        * (2 * SPEED_LIMIT / NVT)
        * (2 * SPEED_LIMIT / NVZ)
        / (2 * math.pi) ** 1.5
    )
    grid_r = speed_grid(NVR)
    grid_t = speed_grid(NVT)
    grid_z = speed_grid(NVZ)
    half_flux = float(
        weight
        * np.sum(np.exp(-(grid_r**2) / 2))
        * np.sum(np.exp(-(grid_t**2) / 2))
        * np.sum(np.maximum(grid_z, 0.0) * np.exp(-(grid_z**2) / 2))
    )
    vel_r = jnp.tile(jnp.asarray(np.repeat(grid_r, NVT), jnp.float32), slot_count)
    vel_t = jnp.tile(jnp.asarray(np.tile(grid_t, NVR), jnp.float32), slot_count)
    slot_speeds = jnp.sum(
        jnp.where(
            z_order[:, None] == jnp.arange(NVZ, dtype=jnp.int32)[None, :],
            jnp.asarray(grid_z, jnp.float32)[None, :],
            0.0,
        ),
        1,
    )
    vel_z = jnp.repeat(slot_speeds, plane_size)
    flat_index = jnp.arange(vdev, dtype=jnp.int32)
    a_index = flat_index // NVT % NVR
    b_index = flat_index % NVT
    speed_sq = vel_r**2 + vel_t**2 + vel_z**2
    maxwell_wall = jnp.exp(-speed_sq / 2)
    element_start = (row_index * row_count).astype(jnp.float32)
    radius = (
        (element_start + jnp.arange(row_count, dtype=jnp.float32))[:, None]
        + (1.0 + jnp.asarray(points, jnp.float32))[None, :] / 2
    ) * ELEMENT_WIDTH
    radius = radius.reshape(local_r)
    code_bottom = jnp.repeat(edge_codes[0], NODES)
    code_top = jnp.repeat(edge_codes[1], NODES)
    down_coef = weight * jnp.maximum(-vel_z, 0.0)
    up_coef = weight * jnp.maximum(vel_z, 0.0)

    def gather_moments(current):
        bottom = jnp.einsum("j,rjv->rv", end_left, current[:, :NODES], precision=HIGHEST_PRECISION)
        top_trace = jnp.einsum(
            "j,rjv->rv", end_right, current[:, local_z - NODES :], precision=HIGHEST_PRECISION
        )
        edge_trace = jnp.where(gz_index == 0, bottom, top_trace)
        first_coef = jnp.where(gz_index == 0, down_coef, up_coef)
        bound_sums = jnp.stack(
            [
                jnp.dot(edge_trace, first_coef, precision=HIGHEST_PRECISION),
                jnp.dot(edge_trace, down_coef, precision=HIGHEST_PRECISION),
            ]
        )
        flat = current.reshape(node_count, vdev)
        moment_basis = jnp.stack(
            [
                jnp.full((vdev,), weight, jnp.float32),
                weight * vel_r,
                weight * vel_t,
                weight * vel_z,
                0.5 * weight * speed_sq,
            ],
            1,
        )
        partials = jnp.dot(
            flat, moment_basis, precision=HIGHEST_PRECISION, preferred_element_type=jnp.float32
        )
        integral_sums_table, bound_sums = lax.psum((partials, bound_sums), "vert")
        particle_concentration = integral_sums_table[:, 0]
        bulk_velocity = integral_sums_table[:, 1:4] / particle_concentration[:, None]
        vapour_warmth = (
            2.0 * integral_sums_table[:, 4] / particle_concentration - jnp.sum(bulk_velocity**2, 1)
        ) / 3.0
        thermal_norm_square = (
            (vel_r[None, :] - bulk_velocity[:, 0:1]) ** 2
            + (vel_t[None, :] - bulk_velocity[:, 1:2]) ** 2
            + (vel_z[None, :] - bulk_velocity[:, 2:3]) ** 2
        )
        weighted = flat * thermal_norm_square
        heat_basis = jnp.stack(
            [
                weight * vel_r,
                weight * vel_t,
                weight * vel_z,
                jnp.full((vdev,), weight, jnp.float32),
            ],
            1,
        )
        heat_parts = jnp.dot(
            weighted, heat_basis, precision=HIGHEST_PRECISION, preferred_element_type=jnp.float32
        )
        heat_local = 0.5 * (heat_parts[:, :3] - bulk_velocity * heat_parts[:, 3:4])
        conduction_integral = lax.psum(heat_local, "vert")
        fluid_observables = (
            particle_concentration,
            bulk_velocity[:, 0],
            bulk_velocity[:, 1],
            bulk_velocity[:, 2],
            vapour_warmth,
            conduction_integral[:, 0],
            conduction_integral[:, 1],
            conduction_integral[:, 2],
        )
        fluid_observables = tuple((entry.reshape(local_r, local_z) for entry in fluid_observables))
        return (fluid_observables, bound_sums)

    def advance(current, fluid_observables, bound_sums):
        (
            particle_concentration,
            drift_outward,
            drift_around,
            drift_lengthwise,
            vapour_warmth,
            conduction_outward,
            conduction_around,
            conduction_lengthwise,
        ) = tuple((entry[:, :, None] for entry in fluid_observables))
        grouped = current.reshape(row_count, NODES, local_z, vdev)
        volume = jnp.einsum("ij,ejzv->eizv", derivative, grouped, precision=HIGHEST_PRECISION)
        trace_hi = jnp.einsum("j,ejzv->ezv", end_right, grouped, precision=HIGHEST_PRECISION)
        trace_lo = jnp.einsum("j,ejzv->ezv", end_left, grouped, precision=HIGHEST_PRECISION)
        mirror = (
            trace_lo[0].reshape(local_z, slot_count, NVR, NVT)[:, :, ::-1, :].reshape(local_z, vdev)
        )
        edge_halo = with_halo(jnp.stack([trace_lo[0], trace_hi[-1]]), (("row", 0),), 1)
        from_left = edge_halo[0]
        from_right = edge_halo[3]
        left_ghost = jnp.where(row_index == 0, mirror, from_left)
        right_ghost = jnp.where(row_index == row_total - 1, trace_hi[-1], from_right)
        plus_side = jnp.concatenate([left_ghost[None], trace_hi], 0)
        minus_side = jnp.concatenate([trace_lo, right_ghost[None]], 0)
        face_values = jnp.where(vel_r > 0, plus_side, minus_side)
        radial = (
            2.0
            / ELEMENT_WIDTH
            * vel_r
            * (
                volume
                + lift_right[None, :, None, None] * (face_values[1:] - trace_hi)[:, None]
                - lift_left[None, :, None, None] * (face_values[:-1] - trace_lo)[:, None]
            )
        )
        radial = radial.reshape(local_r, local_z, vdev)
        grouped = current.reshape(local_r, col_count, NODES, vdev)
        volume = jnp.einsum("ij,rejv->reiv", derivative, grouped, precision=HIGHEST_PRECISION)
        trace_hi = jnp.einsum("j,rejv->rev", end_right, grouped, precision=HIGHEST_PRECISION)
        trace_lo = jnp.einsum("j,rejv->rev", end_left, grouped, precision=HIGHEST_PRECISION)
        edge_halo = with_halo(jnp.stack([trace_lo[:, 0], trace_hi[:, -1]]), (("gz", 0),), 1)
        bottom_density = jnp.where(code_bottom == 1, SAT_DENSITY, bound_sums[0] / half_flux)
        top_density = bound_sums[0] / half_flux
        bottom_ghost = bottom_density[:, None] * maxwell_wall[None, :]
        top_ghost = jnp.where(
            code_top[:, None] == 2, trace_hi[:, -1], top_density[:, None] * maxwell_wall[None, :]
        )
        low_ghost = jnp.where(gz_index == 0, bottom_ghost, edge_halo[0])
        high_ghost = jnp.where(gz_index == gz_total - 1, top_ghost, edge_halo[3])
        plus_side = jnp.concatenate([low_ghost[:, None], trace_hi], 1)
        minus_side = jnp.concatenate([trace_lo, high_ghost[:, None]], 1)
        face_values = jnp.where(vel_z > 0, plus_side, minus_side)
        axial_term = (
            2.0
            / ELEMENT_WIDTH
            * vel_z
            * (
                volume
                + lift_right[None, None, :, None] * (face_values[:, 1:] - trace_hi)[:, :, None]
                - lift_left[None, None, :, None] * (face_values[:, :-1] - trace_lo)[:, :, None]
            )
        )
        axial_term = axial_term.reshape(local_r, local_z, vdev)
        step_r = 2 * SPEED_LIMIT / NVR
        step_t = 2 * SPEED_LIMIT / NVT
        grad_r = (
            shift_velocity(current, NVT, a_index < NVR - 1)
            - shift_velocity(current, -NVT, a_index > 0)
        ) / (2 * step_r)
        grad_t = (
            shift_velocity(current, 1, b_index < NVT - 1) - shift_velocity(current, -1, b_index > 0)
        ) / (2 * step_t)
        rotation = (vel_t * vel_t * grad_r - vel_r * vel_t * grad_t) / radius[:, None, None]
        peculiar_r = vel_r - drift_outward
        peculiar_t = vel_t - drift_around
        peculiar_z = vel_z - drift_lengthwise
        thermal_norm_square = peculiar_r**2 + peculiar_t**2 + peculiar_z**2
        projected_conduction = (
            peculiar_r * conduction_outward
            + peculiar_t * conduction_around
            + peculiar_z * conduction_lengthwise
        )
        gaussian_resting_state = (
            particle_concentration
            * vapour_warmth ** (-1.5)
            * jnp.exp(-thermal_norm_square / (2 * vapour_warmth))
        )
        collision_goal_state = gaussian_resting_state * (
            1.0
            + (1.0 - VISCOUS_RATIO)
            * projected_conduction
            / (5.0 * particle_concentration * vapour_warmth**2)
            * (thermal_norm_square / vapour_warmth - 5.0)
        )
        collide = particle_concentration / KNUDSEN * (collision_goal_state - current)
        return current + TIME_STEP * (collide - radial - axial_term - rotation)

    current = distribution
    for step_index in range(STEPS):
        fluid_observables, bound_sums = gather_moments(current)
        current = advance(current, fluid_observables, bound_sums)
    fluid_observables, bound_sums = gather_moments(current)
    macroscopic = jnp.stack(fluid_observables)
    bottom_row = jnp.where(code_bottom == 1, SAT_DENSITY * half_flux - bound_sums[0], 0.0)
    top_row = jnp.where(code_top == 2, bound_sums[0] - bound_sums[1], 0.0)
    boundary_flux = jnp.where(gz_index == 0, bottom_row, top_row)[None]
    return (current, macroscopic, boundary_flux)


def solution(mesh):
    in_specs = (P("row", "gz", "vert"), P("vert"), P(None, "row"))
    out_specs = (P("row", "gz", "vert"), P(None, "row", "gz"), P("gz", "row"))
    return jax.shard_map(
        on_device, mesh=mesh, in_specs=in_specs, out_specs=out_specs, check_vma=False
    )
```

profile of v0, /device:TPU:27, one launch (start us, length us, event | category | flops | bytes accessed | tf_op | source)
XLA Modules:
  0.0 536.6 jit_solution(1569821555901534045)
XLA Ops:
  0.7 5.3 fusion.58
  10.0 5.0 fusion.150
  25.7 5.5 %fusion.148 = f32[1,16,6912]{2,0,1:T(1,128)} fusion(f32[8,1,1]{0,1,2:T(1,128)S(1)} %copy-done.53, f32[8,16,6912]{2,1,0:T(8,128)S(1)} %copy-done), kind=kOutput, calls=%fused_computation.303 | convolution fusion | flops 10616832 | bytes 3981344 | tf_op jit(solution)/shard_map/j,ejzv->ezv/dot_general | solution.py:264
  31.2 4.1 fusion.158
  35.3 4.1 fusion.157
  56.8 4.4 convolution_bitcast_fusion.4
  61.2 35.3 %psum.63 = f32[128,5]{0,1:T(8,128)} all-reduce(f32[128,5]{0,1:T(8,128)} %convolution_bitcast_fusion.4), channel_id=1, replica_groups=mesh['row'=4,'gz'=2,'vert'=16] {'vert'}, use_global_device_ids=true, to_apply=%region_1.2 | all-reduce | flops 640 | bytes 5120 | tf_op jit(solution)/shard_map/psum | solution.py:212
  99.6 4.7 fusion.83
  131.5 37.9 %all-reduce.10 = (f32[2,8]{1,0:T(2,128)}, f32[128,3]{0,1:T(4,128)}) all-reduce(f32[2,8]{1,0:T(2,128)} %pad_maximum_fusion.1, f32[128,3]{0,1:T(4,128)} %subtract_multiply_fusion.14), channel_id=1, replica_groups=mesh['row'=4,'gz'=2,'vert'=16] {'vert'}, use_global_device_ids=true, to_apply=%region_4.5 | all-reduce | flops 400 | bytes 3200 | tf_op jit(solution)/shard_map/psum | solution.py:212
  181.8 3.8 fusion.60
  196.2 4.2 copy.204
  204.7 3.8 copy.205
  213.7 5.3 collective-permute-done.2
  220.7 3.7 fusion.5
  224.5 3.8 copy.96
  230.8 14.4 %fusion.23 = f32[8,16,6912]{2,0,1:T(8,128)S(1)} fusion(f32[8,16,6912]{2,0,1:T(8,128)} %bitcast.312, f32[8,8,1]{1,0,2:T(8,128)S(1)} %copy-done.105, f32[8,16,6911]{2,0,1:T(8,128)S(1)} %copy.203, f32[8,16,6911]{2,0,1:T(8,128)S(1)} %copy.204, f32[8,16,6864]{2,0,1:T(8,128)} %copy.205, f32[8,16,6864]{2,0,1:T(8,128)S(1)} %copy.206, f32[8]{0:T(128)S(1)} %add_multiply_fusion, ...), kind=kOutput, calls=%fused_computation.27 | convolution fusion | flops 124747776 | bytes 25806688 | tf_op jit(solution)/shard_map/ij,ejzv->eizv/dot_general | solution.py:263
  245.3 4.0 fusion.95
  249.3 4.0 fusion.93
  253.3 4.3 fusion.164
  270.2 4.1 fusion.154
  274.3 4.0 fusion.155
  293.8 5.4 %fusion.162 = f32[128,5]{0,1:T(8,128)} fusion(f32[128,6912]{1,0:T(8,128)} %bitcast.309, f32[6912,5]{0,1:T(8,128)} %stack.24), kind=kOutput, calls=%fused_computation.317 | convolution fusion | flops 53084160 | bytes 3679744 | tf_op jit(solution)/shard_map/dot_general | solution.py:209
  299.2 35.2 %psum.66 = f32[128,5]{0,1:T(8,128)} all-reduce(f32[128,5]{0,1:T(8,128)} %fusion.162), channel_id=1, replica_groups=mesh['row'=4,'gz'=2,'vert'=16] {'vert'}, use_global_device_ids=true, to_apply=%region_5.6 | all-reduce | flops 640 | bytes 5120 | tf_op jit(solution)/shard_map/psum | solution.py:212
  337.7 5.9 %fusion.73 = f32[128,4]{0,1:T(4,128)S(1)} fusion(f32[128,6912]{1,0:T(8,128)} %bitcast.310, f32[128]{0:T(128)S(1)} %get-tuple-element.110, f32[128]{0:T(128)S(1)} %get-tuple-element.109, f32[128]{0:T(128)S(1)} %get-tuple-element.108, f32[6912]{0:T(1024)} %sub.385, f32[6912]{0:T(1024)} %sub.380, f32[6912]{0:T(1024)} %sub.375, f32[6912,1]{0,1:T(1,128)} %broadcast.609, ...), kind=kOutput, calls=%fused_computation.89 | convolution fusion | flops 50512896 | bytes 3736064 | tf_op jit(solution)/shard_map/dot_general | solution.py:233
  366.7 33.9 %all-reduce.9 = (f32[2,8]{1,0:T(2,128)}, f32[128,3]{0,1:T(4,128)}) all-reduce(f32[2,8]{1,0:T(2,128)} %pad_maximum_fusion.2, f32[128,3]{0,1:T(4,128)} %subtract_multiply_fusion.13), channel_id=1, replica_groups=mesh['row'=4,'gz'=2,'vert'=16] {'vert'}, use_global_device_ids=true, to_apply=%region_8.9 | all-reduce | flops 400 | bytes 3200 | tf_op jit(solution)/shard_map/psum | solution.py:212
  417.3 4.3 collective-permute-done.6
  425.2 4.8 fusion.2
  430.0 3.8 copy.115
  436.5 11.2 %fusion.18 = f32[8,16,6912]{2,0,1:T(8,128)S(1)} fusion(f32[8,16,6912]{2,0,1:T(8,128)S(1)} %fusion.23, f32[8,16,6912]{2,0,1:T(8,128)} %bitcast.311, f32[8,8,1]{1,0,2:T(8,128)S(1)} %copy-done.106, f32[8,16,6911]{2,0,1:T(8,128)} %get-tuple-element.57, f32[8,16,6911]{2,0,1:T(8,128)S(1)} %copy-done.22, f32[8,16,6864]{2,0,1:T(8,128)S(1)} %copy-done.21, ...), kind=kOutput, calls=%fused_computation.22 | convolution fusion | flops 124747776 | bytes 25806688 | tf_op jit(solution)/shard_map/ij,ejzv->eizv/dot_general | solution.py:263
  457.7 34.3 %psum.69 = f32[128,5]{0,1:T(8,128)S(1)} all-reduce(f32[128,5]{0,1:T(8,128)S(1)} %fusion.165), channel_id=1, replica_groups=mesh['row'=4,'gz'=2,'vert'=16] {'vert'}, use_global_device_ids=true, to_apply=%region_9.10 | all-reduce | flops 640 | bytes 5120 | tf_op jit(solution)/shard_map/psum | solution.py:212
  493.7 4.7 fusion.63
  501.5 33.2 %all-reduce.8 = (f32[128,3]{0,1:T(4,128)S(1)}, f32[2,8]{1,0:T(2,128)S(1)}) all-reduce(f32[128,3]{0,1:T(4,128)S(1)} %subtract_multiply_fusion.12, f32[2,8]{1,0:T(2,128)S(1)} %pad_maximum_fusion.3), channel_id=1, replica_groups=mesh['row'=4,'gz'=2,'vert'=16] {'vert'}, use_global_device_ids=true, to_apply=%region_11.12 | all-reduce | flops 400 | bytes 3200 | tf_op jit(solution)/shard_map/psum | solution.py:237
  (391 shorter events, 189.9 us)
Async XLA Ops:
  0.6 9.4 %copy-start.56 = (f32[8,1,1]{0,1,2:T(1,128)S(1)}, f32[8,1,1]{0,1,2:T(1,128)}, u32[]{:S(2)}) copy-start(f32[8,1,1]{0,1,2:T(1,128)} %constant.164) | copy-start | bytes 100
  0.6 9.4 %copy-start = (f32[8,16,6912]{2,1,0:T(8,128)S(1)}, f32[8,16,6912]{2,1,0:T(8,128)}, u32[]{:S(2)}) copy-start(f32[8,16,6912]{2,1,0:T(8,128)} %param.12) | copy-start | bytes 10616836
  7.1 16.4 %copy-start.53 = (f32[8,1,1]{0,1,2:T(1,128)S(1)}, f32[8,1,1]{0,1,2:T(1,128)}, u32[]{:S(2)}) copy-start(f32[8,1,1]{0,1,2:T(1,128)} %constant.165) | copy-start | bytes 100
  7.1 202.2 %collective-permute-start.3 = (f32[1,8,6912]{2,0,1:T(1,128)}, f32[1,8,6912]{2,0,1:T(1,128)}, u32[]{:S(2)}, u32[]{:S(2)}) collective-permute-start(f32[1,8,6912]{2,0,1:T(1,128)} %slice_bitcast_fusion.1), channel_id=1, source_target_pairs={{16,0},{17,1},{18,2},{19,3},{20,4},{21,5},{22,6},{23,7},{24,8},{25... | collective-permute-start | bytes 663560 | tf_op jit(solution)/shard_map/ppermute | solution.py:32
  16.6 195.5 %collective-permute-start.1 = (f32[1,16,6912]{2,1,0:T(8,128)}, f32[1,16,6912]{2,1,0:T(8,128)}, u32[]{:S(2)}, u32[]{:S(2)}) collective-permute-start(f32[1,16,6912]{2,1,0:T(8,128)} %copy.216), channel_id=1, source_target_pairs={{32,0},{64,32},{96,64},{33,1},{65,33},{97,65},{34,2},{66,34},{98,6... | collective-permute-start | bytes 1327112 | tf_op jit(solution)/shard_map/ppermute | solution.py:32
  204.7 14.4 %copy-start.97 = (f32[8]{0:T(128)S(1)}, f32[8]{0:T(128)}, u32[]{:S(2)}) copy-start(f32[8]{0:T(128)} %broadcast_select_fusion.14) | copy-start | bytes 100
  204.7 14.6 %copy-start.25 = (f32[1,8,2,6912]{3,2,1,0:T(2,128)S(1)}, f32[1,8,2,6912]{3,2,1,0:T(2,128)}, u32[]{:S(2)}) copy-start(f32[1,8,2,6912]{3,2,1,0:T(2,128)} %copy-done.24) | copy-start | bytes 1327108
  208.5 11.6 %copy-start.9 = (f32[1,8,2,6912]{3,0,2,1:T(1,128)S(1)}, f32[1,8,2,6912]{3,0,2,1:T(1,128)}, u32[]{:S(2)}) copy-start(f32[1,8,2,6912]{3,0,2,1:T(1,128)} %copy-done.8) | copy-start | bytes 1327108
  208.5 11.6 %copy-start.17 = (f32[1,8,2,6912]{3,0,2,1:T(1,128)S(1)}, f32[1,8,2,6912]{3,0,2,1:T(1,128)}, u32[]{:S(2)}) copy-start(f32[1,8,2,6912]{3,0,2,1:T(1,128)} %copy-done.16) | copy-start | bytes 1327108
  209.2 20.8 %copy-start.101 = (f32[8]{0:T(128)}, f32[8]{0:T(128)S(1)}, u32[]{:S(2)}) copy-start(f32[8]{0:T(128)S(1)} %add_multiply_fusion) | copy-start | bytes 100
  210.7 10.0 %copy-start.37 = (f32[6912]{0:T(1024)S(1)}, f32[6912]{0:T(1024)}, u32[]{:S(2)}) copy-start(f32[6912]{0:T(1024)} %get-tuple-element.86) | copy-start | bytes 82948
  210.7 10.0 %copy-start.51 = (f32[8,8,1,1]{1,0,3,2:T(8,128)S(1)}, f32[8,8,1,1]{1,0,3,2:T(8,128)}, u32[]{:S(2)}) copy-start(f32[8,8,1,1]{1,0,3,2:T(8,128)} %constant.166) | copy-start | bytes 772
  210.7 10.0 %copy-start.89 = (f32[8]{0:T(128)S(1)}, f32[8]{0:T(128)}, u32[]{:S(2)}) copy-start(f32[8]{0:T(128)} %constant.131.clone) | copy-start | bytes 100
  210.7 10.0 %copy-start.91 = (f32[8]{0:T(128)S(1)}, f32[8]{0:T(128)}, u32[]{:S(2)}) copy-start(f32[8]{0:T(128)} %constant.130.clone) | copy-start | bytes 100
  210.7 8.3 %collective-permute-start.2 = (f32[1,8,6912]{2,0,1:T(1,128)S(1)}, f32[1,8,6912]{2,0,1:T(1,128)S(1)}, u32[]{:S(2)}, u32[]{:S(2)}) collective-permute-start(f32[1,8,6912]{2,0,1:T(1,128)S(1)} %get-tuple-element.83), channel_id=1, source_target_pairs={{0,16},{1,17},{2,18},{3,19},{4,20},{5,21},{6,22},{7,23},{8,24},{9,... | collective-permute-start | bytes 663560 | tf_op jit(solution)/shard_map/ppermute | solution.py:30
  212.2 16.3 %collective-permute-start = (f32[1,16,6912]{2,1,0:T(8,128)S(1)}, f32[1,16,6912]{2,1,0:T(8,128)S(1)}, u32[]{:S(2)}, u32[]{:S(2)}) collective-permute-start(f32[1,16,6912]{2,1,0:T(8,128)S(1)} %get-tuple-element.79), channel_id=1, source_target_pairs={{0,32},{32,64},{64,96},{1,33},{33,65},{65,97},{2,34},{34,66},{66,9... | collective-permute-start | bytes 1327112 | tf_op jit(solution)/shard_map/ppermute | solution.py:30
  230.8 14.5 %copy-start.94 = (f32[8,1,1,1]{0,1,3,2:T(1,128)S(1)}, f32[8,1,1,1]{0,1,3,2:T(1,128)}, u32[]{:S(2)}) copy-start(f32[8,1,1,1]{0,1,3,2:T(1,128)} %constant.167) | copy-start | bytes 100
  249.3 33.0 %copy-start.12 = (f32[1,8,2,6912]{3,0,2,1:T(1,128)}, f32[1,8,2,6912]{3,0,2,1:T(1,128)S(1)}, u32[]{:S(2)}) copy-start(f32[1,8,2,6912]{3,0,2,1:T(1,128)S(1)} %fusion.95) | copy-start | bytes 1327108
  253.3 25.7 %copy-start.14 = (f32[1,8,2,6912]{3,0,2,1:T(1,128)}, f32[1,8,2,6912]{3,0,2,1:T(1,128)S(1)}, u32[]{:S(2)}) copy-start(f32[1,8,2,6912]{3,0,2,1:T(1,128)S(1)} %fusion.93) | copy-start | bytes 1327108
  260.7 17.5 %copy-start.10 = (f32[1,16,6912]{2,0,1:T(1,128)}, f32[1,16,6912]{2,0,1:T(1,128)S(1)}, u32[]{:S(2)}) copy-start(f32[1,16,6912]{2,0,1:T(1,128)S(1)} %fusion.163) | copy-start | bytes 1327108
  280.1 131.6 %collective-permute-start.7 = (f32[1,8,6912]{2,0,1:T(1,128)}, f32[1,8,6912]{2,0,1:T(1,128)}, u32[]{:S(2)}, u32[]{:S(2)}) collective-permute-start(f32[1,8,6912]{2,0,1:T(1,128)} %slice_bitcast_fusion), channel_id=1, source_target_pairs={{16,0},{17,1},{18,2},{19,3},{20,4},{21,5},{22,6},{23,7},{24,8},{25... | collective-permute-start | bytes 663560 | tf_op jit(solution)/shard_map/ppermute | solution.py:32
  283.3 131.5 %collective-permute-start.5 = (f32[1,16,6912]{2,1,0:T(8,128)}, f32[1,16,6912]{2,1,0:T(8,128)}, u32[]{:S(2)}, u32[]{:S(2)}) collective-permute-start(f32[1,16,6912]{2,1,0:T(8,128)} %copy.215), channel_id=1, source_target_pairs={{32,0},{64,32},{96,64},{33,1},{65,33},{97,65},{34,2},{66,34},{98,6... | collective-permute-start | bytes 1327112 | tf_op jit(solution)/shard_map/ppermute | solution.py:32
  411.0 13.6 %copy-start.13 = (f32[1,8,2,6912]{3,0,2,1:T(1,128)S(1)}, f32[1,8,2,6912]{3,0,2,1:T(1,128)}, u32[]{:S(2)}) copy-start(f32[1,8,2,6912]{3,0,2,1:T(1,128)} %copy-done.12) | copy-start | bytes 1327108
  411.0 13.6 %copy-start.15 = (f32[1,8,2,6912]{3,0,2,1:T(1,128)S(1)}, f32[1,8,2,6912]{3,0,2,1:T(1,128)}, u32[]{:S(2)}) copy-start(f32[1,8,2,6912]{3,0,2,1:T(1,128)} %copy-done.14) | copy-start | bytes 1327108
  413.2 11.9 %copy-start.38 = (f32[6912]{0:T(1024)S(1)}, f32[6912]{0:T(1024)}, u32[]{:S(2)}) copy-start(f32[6912]{0:T(1024)} %get-tuple-element.86) | copy-start | bytes 82948
  413.2 11.9 %copy-start.52 = (f32[8,8,1,1]{1,0,3,2:T(8,128)S(1)}, f32[8,8,1,1]{1,0,3,2:T(8,128)}, u32[]{:S(2)}) copy-start(f32[8,8,1,1]{1,0,3,2:T(8,128)} %constant.166) | copy-start | bytes 772
  413.3 11.9 %copy-start.90 = (f32[8]{0:T(128)S(1)}, f32[8]{0:T(128)}, u32[]{:S(2)}) copy-start(f32[8]{0:T(128)} %constant.131.clone) | copy-start | bytes 100
  413.3 11.9 %copy-start.92 = (f32[8]{0:T(128)S(1)}, f32[8]{0:T(128)}, u32[]{:S(2)}) copy-start(f32[8]{0:T(128)} %constant.130.clone) | copy-start | bytes 100
  413.3 8.4 %collective-permute-start.6 = (f32[1,8,6912]{2,0,1:T(1,128)S(1)}, f32[1,8,6912]{2,0,1:T(1,128)S(1)}, u32[]{:S(2)}, u32[]{:S(2)}) collective-permute-start(f32[1,8,6912]{2,0,1:T(1,128)S(1)} %get-tuple-element.77), channel_id=1, source_target_pairs={{0,16},{1,17},{2,18},{3,19},{4,20},{5,21},{6,22},{7,23},{8,24},{9,... | collective-permute-start | bytes 663560 | tf_op jit(solution)/shard_map/ppermute | solution.py:30
  415.8 18.2 %collective-permute-start.4 = (f32[1,16,6912]{2,1,0:T(8,128)S(1)}, f32[1,16,6912]{2,1,0:T(8,128)S(1)}, u32[]{:S(2)}, u32[]{:S(2)}) collective-permute-start(f32[1,16,6912]{2,1,0:T(8,128)S(1)} %get-tuple-element.73), channel_id=1, source_target_pairs={{0,32},{32,64},{64,96},{1,33},{33,65},{65,97},{2,34},{34,66},{66,9... | collective-permute-start | bytes 1327112 | tf_op jit(solution)/shard_map/ppermute | solution.py:30
  425.2 8.9 %copy-start.28 = (f32[1,16,6912]{2,1,0:T(8,128)S(1)}, f32[1,16,6912]{2,1,0:T(8,128)}, u32[]{:S(2)}) copy-start(f32[1,16,6912]{2,1,0:T(8,128)} %reshape.695) | copy-start | bytes 1327108
  448.9 44.8 %copy-start.5 = (f32[8,16,6912]{2,1,0:T(8,128)}, f32[8,16,6912]{2,1,0:T(8,128)S(1)}, u32[]{:S(2)}) copy-start(f32[8,16,6912]{2,1,0:T(8,128)S(1)} %copy.117) | copy-start | bytes 10616836
  (83 other events, 247.2 us)
where the time goes:
time: 547 us; the launch traced here: 537 us
  blocking collectives  210 us (38%)
  local copies, waits for them, and re-layouts  142 us (26%)
  matrix products  116 us (21%)
  other arithmetic  37.9 us (7%)
  starting transfers between devices  16.4 us (3%)
  waiting for transfers between devices  9.67 us (2%)
    psum x5, blocking collectives, gather_moments(): integral_sums_table, bound_sums = lax.psum((partials, bound_sums), 'vert')  177 us
    psum x1, blocking collectives, gather_moments(): conduction_integral = lax.psum(heat_local, 'vert')  33.2 us
    dot_general x2, matrix products, advance(): jnp.einsum('ij,ejzv->eizv', derivative, grouped, precision=HIGHEST_PRECIS...  25.6 us
    unnamed x231, local copies, waits for them, and re-layouts  20.8 us
    slice x4, local copies, waits for them, and re-layouts, shift_velocity(): shifted = jnp.concatenate([field_entries[..., offset:], padding], -1)  16.2 us
    dot_general x3, matrix products, gather_moments(): jnp.dot(weighted, heat_basis, precision=HIGHEST_PRECISION, preferred_elem...  15.2 us
    dot_general x3, matrix products, gather_moments(): jnp.dot(flat, moment_basis, precision=HIGHEST_PRECISION, preferred_elemen...  12.6 us
  transfers between devices with their start and end apart: 8, of which 2 were waited for; matrix products, arithmetic and copies ran while one was open for 38% of the time, Pallas kernels for 0%

commit v1 on v0

--- a/solution.py
+++ b/solution.py
@@ -234,7 +234,7 @@
             weighted, heat_basis, precision=HIGHEST_PRECISION, preferred_element_type=jnp.float32
         )
         heat_local = 0.5 * (heat_parts[:, :3] - bulk_velocity * heat_parts[:, 3:4])
-        conduction_integral = lax.psum(heat_local, "vert")
+        conduction_integral = jnp.sum(lax.all_gather(heat_local, "vert"), axis=0)
         fluid_observables = (
             particle_concentration,
             bulk_velocity[:, 0],

time: 547 us -> 509 us (0.931)
  the two profiles are of different devices: /device:TPU:27 before, /device:TPU:31 now
where the time goes in v1:
time: 509 us; the launch traced here: 499 us
  blocking collectives  174 us (34%)
  local copies, waits for them, and re-layouts  140 us (28%)
  matrix products  117 us (23%)
  other arithmetic  36.7 us (7%)
  starting transfers between devices  16.6 us (3%)
  waiting for transfers between devices  10.8 us (2%)
    psum x3, blocking collectives, gather_moments(): integral_sums_table, bound_sums = lax.psum((partials, bound_sums), 'vert')  88.7 us
    all_gather x3, blocking collectives, gather_moments(): conduction_integral = jnp.sum(lax.all_gather(heat_local, 'vert'), axis=0)  85.1 us
    dot_general x2, matrix products, advance(): jnp.einsum('ij,ejzv->eizv', derivative, grouped, precision=HIGHEST_PRECIS...  25.6 us
    unnamed x233, local copies, waits for them, and re-layouts  20.8 us
    slice x4, local copies, waits for them, and re-layouts, shift_velocity(): shifted = jnp.concatenate([field_entries[..., offset:], padding], -1)  16.2 us
    dot_general x3, matrix products, gather_moments(): jnp.dot(weighted, heat_basis, precision=HIGHEST_PRECISION, preferred_elem...  15.2 us
    dot_general x3, matrix products, gather_moments(): jnp.dot(flat, moment_basis, precision=HIGHEST_PRECISION, preferred_elemen...  12.7 us
    ppermute x4, starting transfers between devices, with_halo(): lax.ppermute(head, axis, [((i + 1) % count, i) for i in range(ends)])  10.8 us
  transfers between devices with their start and end apart: 8, of which 2 were waited for; matrix products, arithmetic and copies ran while one was open for 41% of the time, Pallas kernels for 0%

profile of v1, /device:TPU:31, one launch (start us, length us, event | category | flops | bytes accessed | tf_op | source)
XLA Modules:
  0.0 499.0 jit_solution(7450444051594437957)
XLA Ops:
  0.7 5.3 %fusion.58 = f32[1,8,2,6912]{3,0,2,1:T(1,128)S(1)} fusion(f32[8,1,1,1]{0,1,3,2:T(1,128)} %constant.168, f32[8,16,6912]{2,1,0:T(8,128)} %param.12), kind=kOutput, calls=%fused_computation.74 | convolution fusion | flops 10616832 | bytes 3981344 | tf_op jit(solution)/shard_map/j,rejv->rev/dot_general | solution.py:291
  10.3 5.0 %fusion.150 = f32[1,16,6912]{2,0,1:T(1,128)S(1)} fusion(f32[8,1,1]{0,1,2:T(1,128)S(1)} %copy-done.56, f32[8,16,6912]{2,1,0:T(8,128)S(1)} %copy-done), kind=kOutput, calls=%fused_computation.308 | convolution fusion | flops 10616832 | bytes 3981344 | tf_op jit(solution)/shard_map/j,ejzv->ezv/dot_general | solution.py:265
  25.9 5.5 %fusion.148 = f32[1,16,6912]{2,0,1:T(1,128)} fusion(f32[8,1,1]{0,1,2:T(1,128)S(1)} %copy-done.53, f32[8,16,6912]{2,1,0:T(8,128)S(1)} %copy-done), kind=kOutput, calls=%fused_computation.306 | convolution fusion | flops 10616832 | bytes 3981344 | tf_op jit(solution)/shard_map/j,ejzv->ezv/dot_general | solution.py:264
  31.5 4.1 fusion.158
  35.5 4.1 fusion.157
  62.9 4.4 convolution_bitcast_fusion.4
  67.9 30.8 %all-reduce.10 = (f32[2,8]{1,0:T(2,128)}, f32[128,5]{0,1:T(8,128)}) all-reduce(f32[2,8]{1,0:T(2,128)} %pad_maximum_fusion.1, f32[128,5]{0,1:T(8,128)} %convolution_bitcast_fusion.4), channel_id=1, replica_groups=mesh['row'=4,'gz'=2,'vert'=16] {'vert'}, use_global_device_ids=true, to_apply=%region_4.5 | all-reduce | flops 656 | bytes 5248 | tf_op jit(solution)/shard_map/psum | solution.py:212
  104.9 4.7 fusion.83
  131.4 29.8 %all-gather = f32[2048,3]{0,1:T(4,128)S(1)} all-gather(f32[128,3]{0,1:T(4,128)} %subtract_multiply_fusion.14), channel_id=2, replica_groups=mesh['row'=4,'gz'=2,'vert'=16] {'vert'}, dimensions={0}, use_global_device_ids=true | all-gather | bytes 26112 | tf_op jit(solution)/shard_map/all_gather | solution.py:237
  169.8 3.8 fusion.60
  184.3 4.2 copy.210
  192.7 3.8 copy.211
  201.8 5.9 %collective-permute-done.2 = f32[1,8,6912]{2,0,1:T(1,128)S(1)} collective-permute-done((f32[1,8,6912]{2,0,1:T(1,128)S(1)}, f32[1,8,6912]{2,0,1:T(1,128)S(1)}, u32[]{:S(2)}, u32[]{:S(2)}) %collective-permute-start.2) | collective-permute-done | bytes 221216 | tf_op jit(solution)/shard_map/ppermute | solution.py:30
  209.3 3.7 fusion.5
  213.1 3.8 copy.96
  219.4 14.4 %fusion.23 = f32[8,16,6912]{2,0,1:T(8,128)S(1)} fusion(f32[8,16,6912]{2,0,1:T(8,128)} %bitcast.327, f32[8,8,1]{1,0,2:T(8,128)S(1)} %copy-done.106, f32[8,16,6911]{2,0,1:T(8,128)S(1)} %copy.209, f32[8,16,6911]{2,0,1:T(8,128)S(1)} %copy.210, f32[8,16,6864]{2,0,1:T(8,128)} %copy.211, f32[8,16,6864]{2,0,1:T(8,128)S(1)} %copy.212, f32[8]{0:T(128)S(1)} %add_multiply_fusion, ...), kind=kOutput, calls=%fused_computation.27 | convolution fusion | flops 124747776 | bytes 25806688 | tf_op jit(solution)/shard_map/ij,ejzv->eizv/dot_general | solution.py:263
  233.9 4.0 fusion.95
  237.9 4.0 fusion.93
  241.9 4.3 fusion.164
  258.7 4.1 fusion.154
  262.8 4.0 fusion.155
  282.3 5.4 %fusion.162 = f32[128,5]{0,1:T(8,128)} fusion(f32[128,6912]{1,0:T(8,128)} %bitcast.324, f32[6912,5]{0,1:T(8,128)} %stack.24), kind=kOutput, calls=%fused_computation.320 | convolution fusion | flops 53084160 | bytes 3679744 | tf_op jit(solution)/shard_map/dot_general | solution.py:209
  288.9 29.3 %all-reduce.9 = (f32[2,8]{1,0:T(2,128)}, f32[128,5]{0,1:T(8,128)}) all-reduce(f32[2,8]{1,0:T(2,128)} %pad_maximum_fusion.2, f32[128,5]{0,1:T(8,128)} %fusion.162), channel_id=1, replica_groups=mesh['row'=4,'gz'=2,'vert'=16] {'vert'}, use_global_device_ids=true, to_apply=%region_8.9 | all-reduce | flops 656 | bytes 5248 | tf_op jit(solution)/shard_map/psum | solution.py:212
  322.6 5.9 %fusion.73 = f32[128,4]{0,1:T(4,128)S(1)} fusion(f32[128,6912]{1,0:T(8,128)} %bitcast.325, f32[128]{0:T(128)S(1)} %get-tuple-element.110, f32[128]{0:T(128)S(1)} %get-tuple-element.109, f32[128]{0:T(128)S(1)} %get-tuple-element.108, f32[6912]{0:T(1024)} %sub.385, f32[6912]{0:T(1024)} %sub.380, f32[6912]{0:T(1024)} %sub.375, f32[6912,1]{0,1:T(1,128)} %broadcast.609, ...), kind=kOutput, calls=%fused_computation.89 | convolution fusion | flops 50512896 | bytes 3736064 | tf_op jit(solution)/shard_map/dot_general | solution.py:233
  350.3 27.5 %all-gather.1 = f32[2048,3]{0,1:T(4,128)S(1)} all-gather(f32[128,3]{0,1:T(4,128)} %subtract_multiply_fusion.13), channel_id=3, replica_groups=mesh['row'=4,'gz'=2,'vert'=16] {'vert'}, dimensions={0}, use_global_device_ids=true | all-gather | bytes 26112 | tf_op jit(solution)/shard_map/all_gather | solution.py:237
  392.5 4.8 collective-permute-done.6
  400.9 4.8 fusion.2
  405.7 3.8 copy.115
  412.3 11.2 %fusion.18 = f32[8,16,6912]{2,0,1:T(8,128)S(1)} fusion(f32[8,16,6912]{2,0,1:T(8,128)S(1)} %fusion.23, f32[8,16,6912]{2,0,1:T(8,128)} %bitcast.326, f32[8,8,1]{1,0,2:T(8,128)S(1)} %copy-done.107, f32[8,16,6911]{2,0,1:T(8,128)} %get-tuple-element.57, f32[8,16,6911]{2,0,1:T(8,128)S(1)} %copy-done.22, f32[8,16,6864]{2,0,1:T(8,128)S(1)} %copy-done.21, ...), kind=kOutput, calls=%fused_computation.22 | convolution fusion | flops 124747776 | bytes 25806688 | tf_op jit(solution)/shard_map/ij,ejzv->eizv/dot_general | solution.py:263
  433.5 28.6 %all-reduce.8 = (f32[128,5]{0,1:T(8,128)S(1)}, f32[2,8]{1,0:T(2,128)S(1)}) all-reduce(f32[128,5]{0,1:T(8,128)S(1)} %fusion.165, f32[2,8]{1,0:T(2,128)S(1)} %pad_maximum_fusion.3), channel_id=1, replica_groups=mesh['row'=4,'gz'=2,'vert'=16] {'vert'}, use_global_device_ids=true, to_apply=%region_9.10 | all-reduce | flops 656 | bytes 5248 | tf_op jit(solution)/shard_map/psum | solution.py:212
  463.2 4.7 fusion.63
  469.7 27.9 %all-gather.2 = f32[2048,3]{0,1:T(4,128)S(1)} all-gather(f32[128,3]{0,1:T(4,128)S(1)} %subtract_multiply_fusion.12), channel_id=4, replica_groups=mesh['row'=4,'gz'=2,'vert'=16] {'vert'}, dimensions={0}, use_global_device_ids=true | all-gather | bytes 26112 | tf_op jit(solution)/shard_map/all_gather | solution.py:237
  (396 shorter events, 187.3 us)
Async XLA Ops:
  0.6 9.7 %copy-start.56 = (f32[8,1,1]{0,1,2:T(1,128)S(1)}, f32[8,1,1]{0,1,2:T(1,128)}, u32[]{:S(2)}) copy-start(f32[8,1,1]{0,1,2:T(1,128)} %constant.164) | copy-start | bytes 100
  0.6 9.7 %copy-start = (f32[8,16,6912]{2,1,0:T(8,128)S(1)}, f32[8,16,6912]{2,1,0:T(8,128)}, u32[]{:S(2)}) copy-start(f32[8,16,6912]{2,1,0:T(8,128)} %param.12) | copy-start | bytes 10616836
  7.1 16.6 %copy-start.53 = (f32[8,1,1]{0,1,2:T(1,128)S(1)}, f32[8,1,1]{0,1,2:T(1,128)}, u32[]{:S(2)}) copy-start(f32[8,1,1]{0,1,2:T(1,128)} %constant.165) | copy-start | bytes 100
  7.1 190.2 %collective-permute-start.3 = (f32[1,8,6912]{2,0,1:T(1,128)}, f32[1,8,6912]{2,0,1:T(1,128)}, u32[]{:S(2)}, u32[]{:S(2)}) collective-permute-start(f32[1,8,6912]{2,0,1:T(1,128)} %slice_bitcast_fusion.1), channel_id=1, source_target_pairs={{16,0},{17,1},{18,2},{19,3},{20,4},{21,5},{22,6},{23,7},{24,8},{25... | collective-permute-start | bytes 663560 | tf_op jit(solution)/shard_map/ppermute | solution.py:32
  16.9 183.3 %collective-permute-start.1 = (f32[1,16,6912]{2,1,0:T(8,128)}, f32[1,16,6912]{2,1,0:T(8,128)}, u32[]{:S(2)}, u32[]{:S(2)}) collective-permute-start(f32[1,16,6912]{2,1,0:T(8,128)} %copy.222), channel_id=1, source_target_pairs={{32,0},{64,32},{96,64},{33,1},{65,33},{97,65},{34,2},{66,34},{98,6... | collective-permute-start | bytes 1327112 | tf_op jit(solution)/shard_map/ppermute | solution.py:32
  192.7 14.9 %copy-start.98 = (f32[8]{0:T(128)S(1)}, f32[8]{0:T(128)}, u32[]{:S(2)}) copy-start(f32[8]{0:T(128)} %broadcast_select_fusion.14) | copy-start | bytes 100
  192.7 15.2 %copy-start.25 = (f32[1,8,2,6912]{3,2,1,0:T(2,128)S(1)}, f32[1,8,2,6912]{3,2,1,0:T(2,128)}, u32[]{:S(2)}) copy-start(f32[1,8,2,6912]{3,2,1,0:T(2,128)} %copy-done.24) | copy-start | bytes 1327108
  196.5 12.1 %copy-start.9 = (f32[1,8,2,6912]{3,0,2,1:T(1,128)S(1)}, f32[1,8,2,6912]{3,0,2,1:T(1,128)}, u32[]{:S(2)}) copy-start(f32[1,8,2,6912]{3,0,2,1:T(1,128)} %copy-done.8) | copy-start | bytes 1327108
  196.5 12.1 %copy-start.17 = (f32[1,8,2,6912]{3,0,2,1:T(1,128)S(1)}, f32[1,8,2,6912]{3,0,2,1:T(1,128)}, u32[]{:S(2)}) copy-start(f32[1,8,2,6912]{3,0,2,1:T(1,128)} %copy-done.16) | copy-start | bytes 1327108
  197.3 21.3 %copy-start.102 = (f32[8]{0:T(128)}, f32[8]{0:T(128)S(1)}, u32[]{:S(2)}) copy-start(f32[8]{0:T(128)S(1)} %add_multiply_fusion) | copy-start | bytes 100
  198.7 10.6 %copy-start.37 = (f32[6912]{0:T(1024)S(1)}, f32[6912]{0:T(1024)}, u32[]{:S(2)}) copy-start(f32[6912]{0:T(1024)} %get-tuple-element.86) | copy-start | bytes 82948
  198.7 10.6 %copy-start.51 = (f32[8,8,1,1]{1,0,3,2:T(8,128)S(1)}, f32[8,8,1,1]{1,0,3,2:T(8,128)}, u32[]{:S(2)}) copy-start(f32[8,8,1,1]{1,0,3,2:T(8,128)} %constant.166) | copy-start | bytes 772
  198.7 10.6 %copy-start.89 = (f32[8]{0:T(128)S(1)}, f32[8]{0:T(128)}, u32[]{:S(2)}) copy-start(f32[8]{0:T(128)} %constant.131.clone) | copy-start | bytes 100
  198.8 10.6 %copy-start.91 = (f32[8]{0:T(128)S(1)}, f32[8]{0:T(128)}, u32[]{:S(2)}) copy-start(f32[8]{0:T(128)} %constant.130.clone) | copy-start | bytes 100
  198.8 8.9 %collective-permute-start.2 = (f32[1,8,6912]{2,0,1:T(1,128)S(1)}, f32[1,8,6912]{2,0,1:T(1,128)S(1)}, u32[]{:S(2)}, u32[]{:S(2)}) collective-permute-start(f32[1,8,6912]{2,0,1:T(1,128)S(1)} %get-tuple-element.83), channel_id=1, source_target_pairs={{0,16},{1,17},{2,18},{3,19},{4,20},{5,21},{6,22},{7,23},{8,24},{9,... | collective-permute-start | bytes 663560 | tf_op jit(solution)/shard_map/ppermute | solution.py:30
  200.3 16.8 %collective-permute-start = (f32[1,16,6912]{2,1,0:T(8,128)S(1)}, f32[1,16,6912]{2,1,0:T(8,128)S(1)}, u32[]{:S(2)}, u32[]{:S(2)}) collective-permute-start(f32[1,16,6912]{2,1,0:T(8,128)S(1)} %get-tuple-element.79), channel_id=1, source_target_pairs={{0,32},{32,64},{64,96},{1,33},{33,65},{65,97},{2,34},{34,66},{66,9... | collective-permute-start | bytes 1327112 | tf_op jit(solution)/shard_map/ppermute | solution.py:30
  219.4 14.5 %copy-start.94 = (f32[8,1,1,1]{0,1,3,2:T(1,128)S(1)}, f32[8,1,1,1]{0,1,3,2:T(1,128)}, u32[]{:S(2)}) copy-start(f32[8,1,1,1]{0,1,3,2:T(1,128)} %constant.167) | copy-start | bytes 100
  237.9 32.9 %copy-start.12 = (f32[1,8,2,6912]{3,0,2,1:T(1,128)}, f32[1,8,2,6912]{3,0,2,1:T(1,128)S(1)}, u32[]{:S(2)}) copy-start(f32[1,8,2,6912]{3,0,2,1:T(1,128)S(1)} %fusion.95) | copy-start | bytes 1327108
  241.9 25.7 %copy-start.14 = (f32[1,8,2,6912]{3,0,2,1:T(1,128)}, f32[1,8,2,6912]{3,0,2,1:T(1,128)S(1)}, u32[]{:S(2)}) copy-start(f32[1,8,2,6912]{3,0,2,1:T(1,128)S(1)} %fusion.93) | copy-start | bytes 1327108
  249.3 17.4 %copy-start.10 = (f32[1,16,6912]{2,0,1:T(1,128)}, f32[1,16,6912]{2,0,1:T(1,128)S(1)}, u32[]{:S(2)}) copy-start(f32[1,16,6912]{2,0,1:T(1,128)S(1)} %fusion.163) | copy-start | bytes 1327108
  268.7 118.3 %collective-permute-start.7 = (f32[1,8,6912]{2,0,1:T(1,128)}, f32[1,8,6912]{2,0,1:T(1,128)}, u32[]{:S(2)}, u32[]{:S(2)}) collective-permute-start(f32[1,8,6912]{2,0,1:T(1,128)} %slice_bitcast_fusion), channel_id=1, source_target_pairs={{16,0},{17,1},{18,2},{19,3},{20,4},{21,5},{22,6},{23,7},{24,8},{25... | collective-permute-start | bytes 663560 | tf_op jit(solution)/shard_map/ppermute | solution.py:32
  271.8 118.1 %collective-permute-start.5 = (f32[1,16,6912]{2,1,0:T(8,128)}, f32[1,16,6912]{2,1,0:T(8,128)}, u32[]{:S(2)}, u32[]{:S(2)}) collective-permute-start(f32[1,16,6912]{2,1,0:T(8,128)} %copy.221), channel_id=1, source_target_pairs={{32,0},{64,32},{96,64},{33,1},{65,33},{97,65},{34,2},{66,34},{98,6... | collective-permute-start | bytes 1327112 | tf_op jit(solution)/shard_map/ppermute | solution.py:32
  386.2 14.0 %copy-start.13 = (f32[1,8,2,6912]{3,0,2,1:T(1,128)S(1)}, f32[1,8,2,6912]{3,0,2,1:T(1,128)}, u32[]{:S(2)}) copy-start(f32[1,8,2,6912]{3,0,2,1:T(1,128)} %copy-done.12) | copy-start | bytes 1327108
  386.2 14.0 %copy-start.15 = (f32[1,8,2,6912]{3,0,2,1:T(1,128)S(1)}, f32[1,8,2,6912]{3,0,2,1:T(1,128)}, u32[]{:S(2)}) copy-start(f32[1,8,2,6912]{3,0,2,1:T(1,128)} %copy-done.14) | copy-start | bytes 1327108
  388.4 12.4 %copy-start.38 = (f32[6912]{0:T(1024)S(1)}, f32[6912]{0:T(1024)}, u32[]{:S(2)}) copy-start(f32[6912]{0:T(1024)} %get-tuple-element.86) | copy-start | bytes 82948
  388.5 12.4 %copy-start.52 = (f32[8,8,1,1]{1,0,3,2:T(8,128)S(1)}, f32[8,8,1,1]{1,0,3,2:T(8,128)}, u32[]{:S(2)}) copy-start(f32[8,8,1,1]{1,0,3,2:T(8,128)} %constant.166) | copy-start | bytes 772
  388.5 12.4 %copy-start.90 = (f32[8]{0:T(128)S(1)}, f32[8]{0:T(128)}, u32[]{:S(2)}) copy-start(f32[8]{0:T(128)} %constant.131.clone) | copy-start | bytes 100
  388.5 12.4 %copy-start.92 = (f32[8]{0:T(128)S(1)}, f32[8]{0:T(128)}, u32[]{:S(2)}) copy-start(f32[8]{0:T(128)} %constant.130.clone) | copy-start | bytes 100
  388.5 8.9 %collective-permute-start.6 = (f32[1,8,6912]{2,0,1:T(1,128)S(1)}, f32[1,8,6912]{2,0,1:T(1,128)S(1)}, u32[]{:S(2)}, u32[]{:S(2)}) collective-permute-start(f32[1,8,6912]{2,0,1:T(1,128)S(1)} %get-tuple-element.77), channel_id=1, source_target_pairs={{0,16},{1,17},{2,18},{3,19},{4,20},{5,21},{6,22},{7,23},{8,24},{9,... | collective-permute-start | bytes 663560 | tf_op jit(solution)/shard_map/ppermute | solution.py:30
  391.0 18.8 %collective-permute-start.4 = (f32[1,16,6912]{2,1,0:T(8,128)S(1)}, f32[1,16,6912]{2,1,0:T(8,128)S(1)}, u32[]{:S(2)}, u32[]{:S(2)}) collective-permute-start(f32[1,16,6912]{2,1,0:T(8,128)S(1)} %get-tuple-element.73), channel_id=1, source_target_pairs={{0,32},{32,64},{64,96},{1,33},{33,65},{65,97},{2,34},{34,66},{66,9... | collective-permute-start | bytes 1327112 | tf_op jit(solution)/shard_map/ppermute | solution.py:30
  400.9 8.9 %copy-start.28 = (f32[1,16,6912]{2,1,0:T(8,128)S(1)}, f32[1,16,6912]{2,1,0:T(8,128)}, u32[]{:S(2)}) copy-start(f32[1,16,6912]{2,1,0:T(8,128)} %reshape.695) | copy-start | bytes 1327108
  424.6 38.6 %copy-start.5 = (f32[8,16,6912]{2,1,0:T(8,128)}, f32[8,16,6912]{2,1,0:T(8,128)S(1)}, u32[]{:S(2)}) copy-start(f32[8,16,6912]{2,1,0:T(8,128)S(1)} %copy.117) | copy-start | bytes 10616836
  (84 other events, 253.1 us)
